TPU v7x, 512 devices: a whole 4x8x8 slice. The times are simulated.
512 devices in a mesh: dp: 32 (over z, x), tensor: 16 (over y, core).
Axes of the slice: x: 4, y: 8, z: 8, core: 2. Of those that a mesh axis runs over, the one named last changes fastest.
Arguments:
- tokens: bfloat16 [16384, 8192], P('dp', 'tensor'), may hold values from -6 to 6
- key_value_weight: bfloat16 [8192, 2048], P('tensor'), may hold values from -0.0625 to 0.0625
- adapter_down_weight: bfloat16 [96, 64, 8192], P('dp', None, 'tensor'), may hold values from -0.0625 to 0.0625
- adapter_up_weight: bfloat16 [96, 64, 2048], P('dp', None, 'tensor'), may hold values from -0.75 to 0.75
- cotangent: bfloat16 [16384, 2048], P('dp', 'tensor'), may hold values from -3 to 3
- sequence_adapter_index: int32 [512], replicated, may hold values from 0 to 95, as said below
- adapter_storage_row: int32 [96], replicated, may hold values from 0 to 95, as said below
Outputs:
- key_value_output: bfloat16 [16384, 2048], P('dp', 'tensor')
- token_gradient: bfloat16 [16384, 8192], P('dp', 'tensor')
- grad_down: float32 [96, 64, 8192], P('dp', None, 'tensor')
- grad_up: float32 [96, 64, 2048], P('dp', None, 'tensor')
Inputs may be any that keep to these rules, and one draw needn't show every extreme that they name: Each value appears once: adapter a is held at row adapter_storage_row[a] of adapter_down_weight, adapter_up_weight, grad_down and grad_up, on index adapter_storage_row[a] // 3 of dp. `sequence_adapter_index`: the 16 sequences i that share one value of i // 16 use adapters held on 16 different indices of dp.
All inputs are finite; a program needn't handle non-finite values.
Results may differ from a plain program's by a relative error of at most 0.02.
Values may be sent and summed in bfloat16 or wider, within the bound.
No kernel may reach another device: no remote copies, remote signals or barrier semaphores. Data moves between devices by JAX's collectives and lax.ppermute only.
A program may use at most 64 MiB of HBM per device.

v0:
```python
import jax
import jax.numpy as jnp
from jax import lax
from jax.sharding import PartitionSpec as P

adapter_scale = 0.25


def gathered_total(value, axis):
    return lax.all_gather(value, axis).astype(jnp.float32).sum(0)


def cut_along(value, dim, length):
    before, after = (value.shape[:dim], value.shape[dim + 1 :])
    return jnp.moveaxis(value.reshape(*before, length, -1, *after), dim, 0)


def sent_and_summed(value, axis, dim):
    pieces = cut_along(value, dim, lax.axis_size(axis))
    arrived = lax.all_to_all(pieces, axis, split_axis=0, concat_axis=0, tiled=True)
    return arrived.astype(jnp.float32).sum(axis=0)


def on_device(
    tokens,
    key_value_weight,
    adapter_down_weight,
    adapter_up_weight,
    cotangent,
    sequence_adapter_index,
    adapter_storage_row,
):
    dp_count = lax.axis_size("dp")
    my_index = lax.axis_index("dp")
    resident_adapters = adapter_down_weight.shape[0]
    rank_span = adapter_down_weight.shape[1]
    block_span = adapter_down_weight.shape[2]
    output_block = adapter_up_weight.shape[2]
    token_row_matrix = tokens.shape[0]
    adapters = adapter_storage_row.shape[0]
    seq_local = sequence_adapter_index.shape[0] // dp_count
    seq_length = token_row_matrix // seq_local
    adapter_codes = jnp.arange(adapters, dtype=jnp.int32)
    matches = sequence_adapter_index[:, None] == adapter_codes[None, :]
    seq_rows = jnp.sum(jnp.where(matches, adapter_storage_row[None, :], 0), axis=1)
    my_rows = lax.dynamic_slice_in_dim(seq_rows, my_index * seq_local, seq_local)
    my_owners = my_rows // resident_adapters
    owner_codes = jnp.arange(dp_count, dtype=jnp.int32)
    from_owner = (my_owners[:, None] == owner_codes[None, :]).astype(jnp.bfloat16)
    reader_rows = seq_rows.reshape(dp_count, seq_local)
    local_codes = jnp.arange(resident_adapters, dtype=jnp.int32) + my_index * resident_adapters
    wanted = (reader_rows[:, :, None] == local_codes[None, None, :]).astype(jnp.float32)
    serve_table = jnp.sum(wanted, axis=1).astype(jnp.bfloat16)
    usage_count = jnp.sum(wanted, axis=(0, 1))
    inverse_use = 1.0 / jnp.maximum(usage_count, 1.0)
    down_flattened = adapter_down_weight.reshape(resident_adapters, rank_span * block_span)
    up_flattened = adapter_up_weight.reshape(resident_adapters, rank_span * output_block)
    send_down = jnp.dot(serve_table, down_flattened, preferred_element_type=jnp.float32).astype(
        jnp.bfloat16
    )
    send_up = jnp.dot(serve_table, up_flattened, preferred_element_type=jnp.float32).astype(
        jnp.bfloat16
    )
    came_down, came_up = (
        lax.all_to_all(send_down, "dp", split_axis=0, concat_axis=0, tiled=True),
        lax.all_to_all(send_up, "dp", split_axis=0, concat_axis=0, tiled=True),
    )
    got_down = jnp.dot(from_owner, came_down, preferred_element_type=jnp.float32)
    got_up = jnp.dot(from_owner, came_up, preferred_element_type=jnp.float32)
    storage_down = got_down.astype(jnp.bfloat16).reshape(seq_local, rank_span, block_span)
    storage_up = got_up.astype(jnp.bfloat16).reshape(seq_local, rank_span, output_block)
    token_sequences = tokens.reshape(seq_local, seq_length, block_span)
    cot_seqs = cotangent.reshape(seq_local, seq_length, output_block)
    inner_part = jnp.einsum(
        "jby,jcy->jbc", token_sequences, storage_down, preferred_element_type=jnp.float32
    )
    back_part = jnp.einsum("slo,sro->slr", cot_seqs, storage_up, preferred_element_type=jnp.float32)
    joined = gathered_total(
        jnp.concatenate([inner_part, back_part], axis=2).astype(jnp.bfloat16), "tensor"
    ).astype(jnp.float32)
    middle_round = joined[:, :, :rank_span].astype(jnp.bfloat16)
    backward_round = joined[:, :, rank_span:].astype(jnp.bfloat16)
    partial_value = jnp.dot(tokens, key_value_weight, preferred_element_type=jnp.float32)
    frozen_backbone = sent_and_summed(partial_value.astype(jnp.bfloat16), "tensor", 1)
    adapter_output = jnp.einsum(
        "ivq,iqg->ivg", middle_round, storage_up, preferred_element_type=jnp.float32
    )
    key_value_output = (
        frozen_backbone + adapter_scale * adapter_output.reshape(token_row_matrix, output_block)
    ).astype(jnp.bfloat16)
    base_gradient = lax.dot_general(
        lax.all_gather(cotangent, "tensor", axis=1, tiled=True),
        key_value_weight,
        (((1,), (1,)), ((), ())),
        preferred_element_type=jnp.float32,
    )
    adapter_gradient = jnp.einsum(
        "cun,cny->cuy", backward_round, storage_down, preferred_element_type=jnp.float32
    )
    token_gradient = (
        base_gradient + adapter_scale * adapter_gradient.reshape(token_row_matrix, block_span)
    ).astype(jnp.bfloat16)
    down_term = (
        adapter_scale
        * jnp.einsum(
            "cfj,cfh->cjh", backward_round, token_sequences, preferred_element_type=jnp.float32
        )
    ).astype(jnp.bfloat16)
    up_term = (
        adapter_scale
        * jnp.einsum("slr,slo->sro", middle_round, cot_seqs, preferred_element_type=jnp.float32)
    ).astype(jnp.bfloat16)
    to_owner = from_owner.T
    ship_down = jnp.dot(
        to_owner, down_term.reshape(seq_local, -1), preferred_element_type=jnp.float32
    ).astype(jnp.bfloat16)
    ship_up = jnp.dot(
        to_owner, up_term.reshape(seq_local, -1), preferred_element_type=jnp.float32
    ).astype(jnp.bfloat16)
    back_down, back_up = (
        lax.all_to_all(ship_down, "dp", split_axis=0, concat_axis=0, tiled=True),
        lax.all_to_all(ship_up, "dp", split_axis=0, concat_axis=0, tiled=True),
    )
    serve_turned = serve_table.T
    grad_down = (
        jnp.dot(serve_turned, back_down, preferred_element_type=jnp.float32) * inverse_use[:, None]
    )
    grad_up = (
        jnp.dot(serve_turned, back_up, preferred_element_type=jnp.float32) * inverse_use[:, None]
    )
    grad_down = grad_down.reshape(resident_adapters, rank_span, block_span)
    grad_up = grad_up.reshape(resident_adapters, rank_span, output_block)
    return (key_value_output, token_gradient, grad_down, grad_up)


def solution(mesh):
    in_specs = (
        P("dp", "tensor"),
        P("tensor", None),
        P("dp", None, "tensor"),
        P("dp", None, "tensor"),
        P("dp", "tensor"),
        P(),
        P(),
    )
    out_specs = (
        P("dp", "tensor"),
        P("dp", "tensor"),
        P("dp", None, "tensor"),
        P("dp", None, "tensor"),
    )
    return jax.shard_map(
        on_device, mesh=mesh, in_specs=in_specs, out_specs=out_specs, check_vma=False
    )
```

profile of v0, /device:TPU:24, one launch (start us, length us, event | category | flops | bytes accessed | tf_op | source)
XLA Modules:
  0.0 297.3 jit_solution(2475872210258353637)
XLA Ops:
  12.4 13.2 %all-to-all-start.2 = ((bf16[32,2,4096]{2,1,0:T(2,128)(2,1)}), bf16[32,2,4096]{2,1,0:T(2,128)(2,1)S(1)}, u32[]{:S(2)}, u32[]{:S(2)}) async-start(bf16[32,2,4096]{2,1,0:T(2,128)(2,1)} %reshape.109), calls=%async_computation.2 | async-start | bytes 1048576 | tf_op jit(solution)/shard_map/all_to_all | solution.py:66
  27.8 4.6 %reduce.2 = bf16[32,32768]{1,0:T(8,128)(2,1)} reduce(bf16[32,1,32768]{2,0,1:T(8,128)(2,1)} %fusion, bf16[]{:T(256)} %broadcast.29), dimensions={1}, to_apply=%copy.23.reduce_sub_computation | reduce | bytes 4194306 | tf_op jit(solution)/shard_map/all_to_all | solution.py:65
  32.4 4.5 %reshape.111 = bf16[32,2,16384]{2,1,0:T(2,128)(2,1)} reshape(bf16[32,32768]{1,0:T(8,128)(2,1)} %reduce.2) | data formatting | bytes 4194304
  36.9 6.4 %all-to-all-done.2 = bf16[32,2,4096]{2,1,0:T(2,128)(2,1)S(1)} async-done(((bf16[32,2,4096]{2,1,0:T(2,128)(2,1)}), bf16[32,2,4096]{2,1,0:T(2,128)(2,1)S(1)}, u32[]{:S(2)}, u32[]{:S(2)}) %all-to-all-start.2) | async-done | bytes 524320 | tf_op jit(solution)/shard_map/all_to_all | solution.py:66
  43.3 4.8 %all-to-all-start.1 = ((bf16[32,2,16384]{2,1,0:T(2,128)(2,1)}), bf16[32,2,16384]{2,1,0:T(2,128)(2,1)}, u32[]{:S(2)}, u32[]{:S(2)}) async-start(bf16[32,2,16384]{2,1,0:T(2,128)(2,1)} %reshape.111), calls=%async_computation.1 | async-start | bytes 4194304 | tf_op jit(solution)/shard_map/all_to_all | solution.py:65
  48.2 3.6 %reshape.110 = bf16[32,1,8192]{2,1,0:T(2,128)(2,1)S(1)} reshape(bf16[32,2,4096]{2,1,0:T(2,128)(2,1)} %copy-done.1) | data formatting | bytes 1048576
  53.5 43.8 %all-to-all-done.1 = bf16[32,2,16384]{2,1,0:T(2,128)(2,1)} async-done(((bf16[32,2,16384]{2,1,0:T(2,128)(2,1)}), bf16[32,2,16384]{2,1,0:T(2,128)(2,1)}, u32[]{:S(2)}, u32[]{:S(2)}) %all-to-all-start.1) | async-done | bytes 2097184 | tf_op jit(solution)/shard_map/all_to_all | solution.py:65
  97.3 10.5 %reshape.112 = bf16[32,1,32768]{2,1,0:T(2,128)(2,1)} reshape(bf16[32,2,16384]{2,1,0:T(2,128)(2,1)} %all-to-all-done.1) | data formatting | bytes 4194304
  107.8 4.6 %convolution_convert_fusion.2 = bf16[16,32768]{1,0:T(8,128)(2,1)S(1)} fusion(bf16[32,1,32768]{2,1,0:T(2,128)(2,1)} %reshape.112, s32[16]{0:T(128)S(1)} %and_select_fusion), kind=kOutput, calls=%fused_computation.4 | convolution fusion | flops 34079232 | bytes 3145792 | tf_op jit(solution)/shard_map/dot_general | solution.py:68
  114.0 2.3 fusion.8
  118.2 7.3 %all-to-all-start = ((bf16[16,512,128]{2,1,0:T(8,128)(2,1)}), bf16[16,512,128]{2,1,0:T(8,128)(2,1)}, u32[]{:S(2)}, u32[]{:S(2)}) async-start(bf16[16,512,128]{2,1,0:T(8,128)(2,1)} %bitcast.89), calls=%async_computation | async-start | bytes 4194304 | tf_op jit(solution)/shard_map/all_to_all | solution.py:20
  125.5 54.0 %all-gather.3.cloned.1.call-done = bf16[16,16,32,128]{3,2,1,0:T(8,128)(2,1)} async-done(((bf16[1,16,32,128]{3,2,1,0:T(8,128)(2,1)}), bf16[16,16,32,128]{3,2,1,0:T(8,128)(2,1)}) %all-gather.3.cloned.1.call-update) | async-done | bytes 2097168 | tf_op jit(solution)/shard_map/all_gather | solution.py:10
  183.8 2.7 reduce.4
  188.8 11.6 %all-to-all-start.4 = ((bf16[32,2,4096]{2,1,0:T(2,128)(2,1)}), bf16[32,2,4096]{2,1,0:T(2,128)(2,1)}, u32[]{:S(2)}, u32[]{:S(2)}) async-start(bf16[32,2,4096]{2,1,0:T(2,128)(2,1)} %reshape.115), calls=%async_computation.4 | async-start | bytes 1048576 | tf_op jit(solution)/shard_map/all_to_all | solution.py:122
  205.7 4.5 %reduce.3 = bf16[32,32768]{1,0:T(8,128)(2,1)} reduce(bf16[32,1,32768]{2,0,1:T(8,128)(2,1)} %fusion.1, bf16[]{:T(256)} %broadcast.29), dimensions={1}, to_apply=%copy.25.reduce_sub_computation | reduce | bytes 4194306 | tf_op jit(solution)/shard_map/all_to_all | solution.py:121
  210.3 4.5 %reshape.113 = bf16[32,2,16384]{2,1,0:T(2,128)(2,1)} reshape(bf16[32,32768]{1,0:T(8,128)(2,1)} %reduce.3) | data formatting | bytes 4194304
  214.8 3.8 %all-to-all-done.4 = bf16[32,2,4096]{2,1,0:T(2,128)(2,1)} async-done(((bf16[32,2,4096]{2,1,0:T(2,128)(2,1)}), bf16[32,2,4096]{2,1,0:T(2,128)(2,1)}, u32[]{:S(2)}, u32[]{:S(2)}) %all-to-all-start.4) | async-done | bytes 524320 | tf_op jit(solution)/shard_map/all_to_all | solution.py:122
  218.6 6.0 %all-to-all-start.3 = ((bf16[32,2,16384]{2,1,0:T(2,128)(2,1)}), bf16[32,2,16384]{2,1,0:T(2,128)(2,1)}, u32[]{:S(2)}, u32[]{:S(2)}) async-start(bf16[32,2,16384]{2,1,0:T(2,128)(2,1)} %reshape.113), calls=%async_computation.3 | async-start | bytes 4194304 | tf_op jit(solution)/shard_map/all_to_all | solution.py:121
  228.8 16.4 %all-gather.5.cloned.1.call-done = bf16[512,2048]{1,0:T(8,128)(2,1)} async-done(((bf16[512,128]{1,0:T(8,128)(2,1)}), bf16[512,2048]{1,0:T(8,128)(2,1)}) %all-gather.5.cloned.1.call-update) | async-done | bytes 2097168 | tf_op jit(solution)/shard_map/all_gather | solution.py:92
  245.2 3.9 %fusion.9 = bf16[512,512]{1,0:T(8,128)(2,1)} fusion(f32[512,512]{1,0:T(8,128)} %bitcast.101, bf16[512,2048]{1,0:T(8,128)(2,1)} %all-gather.5.cloned.1.call-done, bf16[512,2048]{1,0:T(8,128)(2,1)S(1)} %copy-done), kind=kOutput, calls=%fused_computation.23 | convolution fusion | flops 1074266112 | bytes 5767168 | tf_op jit(solution)/shard_map/dot_general | solution.py:91
  249.1 3.6 %reshape.116 = bf16[32,1,8192]{2,1,0:T(2,128)(2,1)S(1)} reshape(bf16[32,2,4096]{2,1,0:T(2,128)(2,1)} %all-to-all-done.4) | data formatting | bytes 1048576
  254.1 20.5 %all-to-all-done.3 = bf16[32,2,16384]{2,1,0:T(2,128)(2,1)} async-done(((bf16[32,2,16384]{2,1,0:T(2,128)(2,1)}), bf16[32,2,16384]{2,1,0:T(2,128)(2,1)}, u32[]{:S(2)}, u32[]{:S(2)}) %all-to-all-start.3) | async-done | bytes 2097184 | tf_op jit(solution)/shard_map/all_to_all | solution.py:121
  274.6 10.5 %reshape.114 = bf16[32,1,32768]{2,1,0:T(2,128)(2,1)} reshape(bf16[32,2,16384]{2,1,0:T(2,128)(2,1)} %all-to-all-done.3) | data formatting | bytes 4194304
  285.0 4.5 %convolution_multiply_fusion = f32[3,32768]{1,0:T(4,128)S(1)} fusion(bf16[32,3]{0,1:T(4,128)(2,1)S(1)} %get-tuple-element.5, bf16[32,1,32768]{2,1,0:T(2,128)(2,1)} %reshape.114, f32[3]{0:T(128)S(1)} %maximum_divide_fusion), kind=kOutput, calls=%fused_computation.5 | convolution fusion | flops 6389760 | bytes 2490572 | tf_op jit(solution)/shard_map/dot_general | solution.py:126
  (51 shorter events, 30.9 us)
Async XLA Ops:
  7.2 106.9 %copy-start = (bf16[512,2048]{1,0:T(8,128)(2,1)S(1)}, bf16[512,2048]{1,0:T(8,128)(2,1)}, u32[]{:S(2)}) copy-start(bf16[512,2048]{1,0:T(8,128)(2,1)} %param.8) | copy-start | bytes 6291460
  7.2 18.4 %copy-start.5 = (bf16[3,64,512]{2,1,0:T(8,128)(2,1)S(1)}, bf16[3,64,512]{2,1,0:T(8,128)(2,1)}, u32[]{:S(2)}) copy-start(bf16[3,64,512]{2,1,0:T(8,128)(2,1)} %param.9) | copy-start | bytes 589828
  12.4 30.9 %all-to-all-start.2 = ((bf16[32,2,4096]{2,1,0:T(2,128)(2,1)}), bf16[32,2,4096]{2,1,0:T(2,128)(2,1)S(1)}, u32[]{:S(2)}, u32[]{:S(2)}) async-start(bf16[32,2,4096]{2,1,0:T(2,128)(2,1)} %reshape.109), calls=%async_computation.2 | async-start | bytes 1048576 | tf_op jit(solution)/shard_map/all_to_all | solution.py:66
  43.3 4.9 %copy-start.1 = (bf16[32,2,4096]{2,1,0:T(2,128)(2,1)}, bf16[32,2,4096]{2,1,0:T(2,128)(2,1)S(1)}, u32[]{:S(2)}) copy-start(bf16[32,2,4096]{2,1,0:T(2,128)(2,1)S(1)} %all-to-all-done.2) | copy-start | bytes 1572868
  43.3 54.0 %all-to-all-start.1 = ((bf16[32,2,16384]{2,1,0:T(2,128)(2,1)}), bf16[32,2,16384]{2,1,0:T(2,128)(2,1)}, u32[]{:S(2)}, u32[]{:S(2)}) async-start(bf16[32,2,16384]{2,1,0:T(2,128)(2,1)} %reshape.111), calls=%async_computation.1 | async-start | bytes 4194304 | tf_op jit(solution)/shard_map/all_to_all | solution.py:65
  48.1 4.5 %copy-start.3 = (bf16[512,128]{1,0:T(8,128)(2,1)S(1)}, bf16[512,128]{1,0:T(8,128)(2,1)}, u32[]{:S(2)}) copy-start(bf16[512,128]{1,0:T(8,128)(2,1)} %param.11) | copy-start | bytes 393220
  48.1 131.4 %all-gather.3.cloned.1.call-start = ((), (), s32[]{:S(2)}) async-start(), calls=%async_computation.5 | async-start | bytes 2228224 | tf_op jit(solution)/shard_map/all_gather | solution.py:10
  107.8 4.9 %copy-start.2 = (bf16[512,512]{1,0:T(8,128)(2,1)S(1)}, bf16[512,512]{1,0:T(8,128)(2,1)}, u32[]{:S(2)}) copy-start(bf16[512,512]{1,0:T(8,128)(2,1)} %param.7) | copy-start | bytes 1572868
  112.3 0.9 copy-start.4
  118.2 70.6 %all-to-all-start = ((bf16[16,512,128]{2,1,0:T(8,128)(2,1)}), bf16[16,512,128]{2,1,0:T(8,128)(2,1)}, u32[]{:S(2)}, u32[]{:S(2)}) async-start(bf16[16,512,128]{2,1,0:T(8,128)(2,1)} %bitcast.89), calls=%async_computation | async-start | bytes 4194304 | tf_op jit(solution)/shard_map/all_to_all | solution.py:20
  188.8 29.8 %all-to-all-start.4 = ((bf16[32,2,4096]{2,1,0:T(2,128)(2,1)}), bf16[32,2,4096]{2,1,0:T(2,128)(2,1)}, u32[]{:S(2)}, u32[]{:S(2)}) async-start(bf16[32,2,4096]{2,1,0:T(2,128)(2,1)} %reshape.115), calls=%async_computation.4 | async-start | bytes 1048576 | tf_op jit(solution)/shard_map/all_to_all | solution.py:122
  200.4 44.8 %all-gather.5.cloned.1.call-start = ((), (), s32[]{:S(2)}) async-start(), calls=%async_computation.6 | async-start | bytes 2228224 | tf_op jit(solution)/shard_map/all_gather | solution.py:92
  218.6 56.0 %all-to-all-start.3 = ((bf16[32,2,16384]{2,1,0:T(2,128)(2,1)}), bf16[32,2,16384]{2,1,0:T(2,128)(2,1)}, u32[]{:S(2)}, u32[]{:S(2)}) async-start(bf16[32,2,16384]{2,1,0:T(2,128)(2,1)} %reshape.113), calls=%async_computation.3 | async-start | bytes 4194304 | tf_op jit(solution)/shard_map/all_to_all | solution.py:121
Sparse Core Ops, SparseCore 0:
  114.2 65.3 all-gather.2
  203.3 41.8 all-gather.4
where the time goes:
time: 299 us; the launch traced here: 297 us
  waiting for transfers between devices  146 us (49%)
  local copies, waits for them, and re-layouts  45.9 us (15%)
  starting transfers between devices  43 us (14%)
  matrix products  29.1 us (10%)
  other arithmetic  19.4 us (6%)
  between operations  14.2 us (5%)
    all_gather x1, waiting for transfers between devices, gathered_total(): return lax.all_gather(value, axis).astype(jnp.float32).sum(0)  54 us
    all_to_all x1, waiting for transfers between devices, on_device(): lax.all_to_all(send_down, 'dp', split_axis=0, concat_axis=0, tiled=True)  43.8 us
    unnamed x26, local copies, waits for them, and re-layouts  43.4 us
    all_to_all x1, waiting for transfers between devices, on_device(): lax.all_to_all(ship_down, 'dp', split_axis=0, concat_axis=0, tiled=True)  20.5 us
    all_gather x1, waiting for transfers between devices, on_device(): lax.all_gather(cotangent, 'tensor', axis=1, tiled=True)  16.4 us
    all_to_all x1, starting transfers between devices, on_device(): lax.all_to_all(send_up, 'dp', split_axis=0, concat_axis=0, tiled=True)  13.2 us
    all_to_all x1, starting transfers between devices, on_device(): lax.all_to_all(ship_up, 'dp', split_axis=0, concat_axis=0, tiled=True)  11.6 us
    all_to_all x1, starting transfers between devices, sent_and_summed(): lax.all_to_all(pieces, axis, split_axis=0, concat_axis=0, tiled=True)  7.34 us
  transfers between devices with their start and end apart: 7, of which 6 were waited for; matrix products, arithmetic and copies ran while one was open for 19% of the time, Pallas kernels for 0%

commit v1 on v0

--- a/solution.py
+++ b/solution.py
@@ -89,7 +89,9 @@
         frozen_backbone + adapter_scale * adapter_output.reshape(token_row_matrix, output_block)
     ).astype(jnp.bfloat16)
     base_gradient = lax.dot_general(
-        lax.all_gather(cotangent, "tensor", axis=1, tiled=True),
+        jnp.concatenate(
+            lax.all_to_all(jnp.stack([cotangent] * lax.axis_size("tensor")), "tensor", 0, 0), axis=1
+        ),
         key_value_weight,
         (((1,), (1,)), ((), ())),
         preferred_element_type=jnp.float32,

time: 299 us -> 319 us (1.067)
  the two profiles are of different devices: /device:TPU:24 before, /device:TPU:4 now
where the time goes in v1:
time: 319 us; the launch traced here: 317 us
  waiting for transfers between devices  165 us (52%)
  local copies, waits for them, and re-layouts  49.1 us (15%)
  starting transfers between devices  42.7 us (13%)
  matrix products  26.8 us (8%)
  other arithmetic  19.3 us (6%)
  between operations  14.3 us (4%)
    all_to_all x1, waiting for transfers between devices, on_device(): lax.all_to_all(send_down, 'dp', split_axis=0, concat_axis=0, tiled=True)  46.5 us
    unnamed x29, local copies, waits for them, and re-layouts  44.2 us
    all_to_all x1, waiting for transfers between devices, on_device(): lax.all_to_all(ship_down, 'dp', split_axis=0, concat_axis=0, tiled=True)  37.6 us
    all_to_all x1, waiting for transfers between devices, sent_and_summed(): lax.all_to_all(pieces, axis, split_axis=0, concat_axis=0, tiled=True)  31.3 us
    all_to_all x1, waiting for transfers between devices, on_device(): lax.all_to_all(jnp.stack([cotangent] * lax.axis_size('tensor')), 'tensor'...  27.9 us
    all_to_all x1, starting transfers between devices, on_device(): lax.all_to_all(send_up, 'dp', split_axis=0, concat_axis=0, tiled=True)  13.4 us
    all_gather x1, waiting for transfers between devices, gathered_total(): return lax.all_gather(value, axis).astype(jnp.float32).sum(0)  12.8 us
    all_to_all x1, starting transfers between devices, sent_and_summed(): lax.all_to_all(pieces, axis, split_axis=0, concat_axis=0, tiled=True)  7.26 us
  transfers between devices with their start and end apart: 7, of which 7 were waited for; matrix products, arithmetic and copies ran while one was open for 23% of the time, Pallas kernels for 0%

profile of v1, /device:TPU:4, one launch (start us, length us, event | category | flops | bytes accessed | tf_op | source)
XLA Modules:
  0.0 317.1 jit_solution(8084375405574795370)
XLA Ops:
  12.4 13.4 %all-to-all-start.2 = ((bf16[32,2,4096]{2,1,0:T(2,128)(2,1)}), bf16[32,2,4096]{2,1,0:T(2,128)(2,1)S(1)}, u32[]{:S(2)}, u32[]{:S(2)}) async-start(bf16[32,2,4096]{2,1,0:T(2,128)(2,1)} %reshape.119), calls=%async_computation.2 | async-start | bytes 1048576 | tf_op jit(solution)/shard_map/all_to_all | solution.py:66
  28.1 4.5 %reduce.2 = bf16[32,32768]{1,0:T(8,128)(2,1)} reduce(bf16[32,1,32768]{2,0,1:T(8,128)(2,1)} %fusion, bf16[]{:T(256)} %broadcast.31), dimensions={1}, to_apply=%copy.26.reduce_sub_computation | reduce | bytes 4194306 | tf_op jit(solution)/shard_map/all_to_all | solution.py:65
  32.6 4.5 %reshape.121 = bf16[32,2,16384]{2,1,0:T(2,128)(2,1)} reshape(bf16[32,32768]{1,0:T(8,128)(2,1)} %reduce.2) | data formatting | bytes 4194304
  37.1 5.5 %all-to-all-done.2 = bf16[32,2,4096]{2,1,0:T(2,128)(2,1)S(1)} async-done(((bf16[32,2,4096]{2,1,0:T(2,128)(2,1)}), bf16[32,2,4096]{2,1,0:T(2,128)(2,1)S(1)}, u32[]{:S(2)}, u32[]{:S(2)}) %all-to-all-start.2) | async-done | bytes 524320 | tf_op jit(solution)/shard_map/all_to_all | solution.py:66
  42.6 5.6 %all-to-all-start.1 = ((bf16[32,2,16384]{2,1,0:T(2,128)(2,1)}), bf16[32,2,16384]{2,1,0:T(2,128)(2,1)}, u32[]{:S(2)}, u32[]{:S(2)}) async-start(bf16[32,2,16384]{2,1,0:T(2,128)(2,1)} %reshape.121), calls=%async_computation.1 | async-start | bytes 4194304 | tf_op jit(solution)/shard_map/all_to_all | solution.py:65
  51.5 46.5 %all-to-all-done.1 = bf16[32,2,16384]{2,1,0:T(2,128)(2,1)} async-done(((bf16[32,2,16384]{2,1,0:T(2,128)(2,1)}), bf16[32,2,16384]{2,1,0:T(2,128)(2,1)}, u32[]{:S(2)}, u32[]{:S(2)}) %all-to-all-start.1) | async-done | bytes 2097184 | tf_op jit(solution)/shard_map/all_to_all | solution.py:65
  98.0 7.3 %all-to-all-start = ((bf16[16,512,128]{2,1,0:T(8,128)(2,1)}), bf16[16,512,128]{2,1,0:T(8,128)(2,1)}, u32[]{:S(2)}, u32[]{:S(2)}) async-start(bf16[16,512,128]{2,1,0:T(8,128)(2,1)} %bitcast.92), calls=%async_computation | async-start | bytes 4194304 | tf_op jit(solution)/shard_map/all_to_all | solution.py:20
  105.4 3.6 %reshape.120 = bf16[32,1,8192]{2,1,0:T(2,128)(2,1)S(1)} reshape(bf16[32,2,4096]{2,1,0:T(2,128)(2,1)} %copy-done.1) | data formatting | bytes 1048576
  110.6 10.5 %reshape.122 = bf16[32,1,32768]{2,1,0:T(2,128)(2,1)} reshape(bf16[32,2,16384]{2,1,0:T(2,128)(2,1)} %all-to-all-done.1) | data formatting | bytes 4194304
  121.1 4.6 %convolution_convert_fusion.2 = bf16[16,32768]{1,0:T(8,128)(2,1)S(1)} fusion(bf16[32,1,32768]{2,1,0:T(2,128)(2,1)} %reshape.122, s32[16]{0:T(128)S(1)} %and_select_fusion), kind=kOutput, calls=%fused_computation.4 | convolution fusion | flops 34079232 | bytes 3145792 | tf_op jit(solution)/shard_map/dot_general | solution.py:68
  128.1 31.3 %all-to-all-done = bf16[16,512,128]{2,1,0:T(8,128)(2,1)} async-done(((bf16[16,512,128]{2,1,0:T(8,128)(2,1)}), bf16[16,512,128]{2,1,0:T(8,128)(2,1)}, u32[]{:S(2)}, u32[]{:S(2)}) %all-to-all-start) | async-done | bytes 2097184 | tf_op jit(solution)/shard_map/all_to_all | solution.py:20
  161.8 4.6 %all-to-all-start.3 = ((bf16[16,512,128]{1,2,0:T(8,128)(2,1)}), bf16[16,512,128]{1,2,0:T(8,128)(2,1)}, u32[]{:S(2)}, u32[]{:S(2)}) async-start(bf16[16,512,128]{1,2,0:T(8,128)(2,1)} %stack.2), calls=%async_computation.3 | async-start | bytes 4194304 | tf_op jit(solution)/shard_map/all_to_all | solution.py:93
  166.5 12.8 %all-gather.2.cloned.1.call-done = bf16[16,16,32,128]{3,2,1,0:T(8,128)(2,1)} async-done(((bf16[1,16,32,128]{3,2,1,0:T(8,128)(2,1)}), bf16[16,16,32,128]{3,2,1,0:T(8,128)(2,1)}) %all-gather.2.cloned.1.call-update) | async-done | bytes 2097168 | tf_op jit(solution)/shard_map/all_gather | solution.py:10
  188.5 27.9 %all-to-all-done.3 = bf16[16,512,128]{1,2,0:T(8,128)(2,1)} async-done(((bf16[16,512,128]{1,2,0:T(8,128)(2,1)}), bf16[16,512,128]{1,2,0:T(8,128)(2,1)}, u32[]{:S(2)}, u32[]{:S(2)}) %all-to-all-start.3) | async-done | bytes 2097184 | tf_op jit(solution)/shard_map/all_to_all | solution.py:93
  216.4 5.2 %all-to-all-start.5 = ((bf16[32,2,4096]{2,1,0:T(2,128)(2,1)}), bf16[32,2,4096]{2,1,0:T(2,128)(2,1)}, u32[]{:S(2)}, u32[]{:S(2)}) async-start(bf16[32,2,4096]{2,1,0:T(2,128)(2,1)} %reshape.125), calls=%async_computation.5 | async-start | bytes 1048576 | tf_op jit(solution)/shard_map/all_to_all | solution.py:124
  226.1 4.6 %reduce.3 = bf16[32,32768]{1,0:T(8,128)(2,1)} reduce(bf16[32,1,32768]{2,0,1:T(8,128)(2,1)} %fusion.1, bf16[]{:T(256)} %broadcast.31), dimensions={1}, to_apply=%copy.29.reduce_sub_computation | reduce | bytes 4194306 | tf_op jit(solution)/shard_map/all_to_all | solution.py:123
  230.7 4.5 %reshape.123 = bf16[32,2,16384]{2,1,0:T(2,128)(2,1)} reshape(bf16[32,32768]{1,0:T(8,128)(2,1)} %reduce.3) | data formatting | bytes 4194304
  235.2 3.3 %all-to-all-done.5 = bf16[32,2,4096]{2,1,0:T(2,128)(2,1)} async-done(((bf16[32,2,4096]{2,1,0:T(2,128)(2,1)}), bf16[32,2,4096]{2,1,0:T(2,128)(2,1)}, u32[]{:S(2)}, u32[]{:S(2)}) %all-to-all-start.5) | async-done | bytes 524320 | tf_op jit(solution)/shard_map/all_to_all | solution.py:124
  238.5 6.5 %all-to-all-start.4 = ((bf16[32,2,16384]{2,1,0:T(2,128)(2,1)}), bf16[32,2,16384]{2,1,0:T(2,128)(2,1)}, u32[]{:S(2)}, u32[]{:S(2)}) async-start(bf16[32,2,16384]{2,1,0:T(2,128)(2,1)} %reshape.123), calls=%async_computation.4 | async-start | bytes 4194304 | tf_op jit(solution)/shard_map/all_to_all | solution.py:123
  248.2 3.7 %fusion.9 = bf16[512,512]{1,0:T(8,128)(2,1)} fusion(f32[512,512]{1,0:T(8,128)S(1)} %bitcast.104, bf16[512,2048]{0,1:T(8,128)(2,1)} %bitcast.11, bf16[512,2048]{1,0:T(8,128)(2,1)S(1)} %copy-done), kind=kOutput, calls=%fused_computation.23 | convolution fusion | flops 1074266112 | bytes 5767168 | tf_op jit(solution)/shard_map/dot_general | solution.py:91
  251.9 3.6 %reshape.126 = bf16[32,1,8192]{2,1,0:T(2,128)(2,1)S(1)} reshape(bf16[32,2,4096]{2,1,0:T(2,128)(2,1)} %all-to-all-done.5) | data formatting | bytes 1048576
  256.9 37.6 %all-to-all-done.4 = bf16[32,2,16384]{2,1,0:T(2,128)(2,1)} async-done(((bf16[32,2,16384]{2,1,0:T(2,128)(2,1)}), bf16[32,2,16384]{2,1,0:T(2,128)(2,1)}, u32[]{:S(2)}, u32[]{:S(2)}) %all-to-all-start.4) | async-done | bytes 2097184 | tf_op jit(solution)/shard_map/all_to_all | solution.py:123
  294.4 10.5 %reshape.124 = bf16[32,1,32768]{2,1,0:T(2,128)(2,1)} reshape(bf16[32,2,16384]{2,1,0:T(2,128)(2,1)} %all-to-all-done.4) | data formatting | bytes 4194304
  304.9 4.5 %convolution_multiply_fusion = f32[3,32768]{1,0:T(4,128)S(1)} fusion(bf16[32,3]{0,1:T(4,128)(2,1)S(1)} %get-tuple-element.5, bf16[32,1,32768]{2,1,0:T(2,128)(2,1)} %reshape.124, f32[3]{0:T(128)S(1)} %maximum_divide_fusion), kind=kOutput, calls=%fused_computation.5 | convolution fusion | flops 6389760 | bytes 2490572 | tf_op jit(solution)/shard_map/dot_general | solution.py:128
  (54 shorter events, 36.3 us)
Async XLA Ops:
  7.2 41.1 %copy-start = (bf16[512,2048]{1,0:T(8,128)(2,1)S(1)}, bf16[512,2048]{1,0:T(8,128)(2,1)}, u32[]{:S(2)}) copy-start(bf16[512,2048]{1,0:T(8,128)(2,1)} %param.8) | copy-start | bytes 6291460
  7.2 18.6 %copy-start.6 = (bf16[3,64,512]{2,1,0:T(8,128)(2,1)S(1)}, bf16[3,64,512]{2,1,0:T(8,128)(2,1)}, u32[]{:S(2)}) copy-start(bf16[3,64,512]{2,1,0:T(8,128)(2,1)} %param.9) | copy-start | bytes 589828
  12.4 30.3 %all-to-all-start.2 = ((bf16[32,2,4096]{2,1,0:T(2,128)(2,1)}), bf16[32,2,4096]{2,1,0:T(2,128)(2,1)S(1)}, u32[]{:S(2)}, u32[]{:S(2)}) async-start(bf16[32,2,4096]{2,1,0:T(2,128)(2,1)} %reshape.119), calls=%async_computation.2 | async-start | bytes 1048576 | tf_op jit(solution)/shard_map/all_to_all | solution.py:66
  37.1 11.2 %copy-start.2 = (bf16[512,512]{1,0:T(8,128)(2,1)S(1)}, bf16[512,512]{1,0:T(8,128)(2,1)}, u32[]{:S(2)}) copy-start(bf16[512,512]{1,0:T(8,128)(2,1)} %param.7) | copy-start | bytes 1572868
  42.6 6.9 %copy-start.1 = (bf16[32,2,4096]{2,1,0:T(2,128)(2,1)}, bf16[32,2,4096]{2,1,0:T(2,128)(2,1)S(1)}, u32[]{:S(2)}) copy-start(bf16[32,2,4096]{2,1,0:T(2,128)(2,1)S(1)} %all-to-all-done.2) | copy-start | bytes 1572868
  42.6 55.3 %all-to-all-start.1 = ((bf16[32,2,16384]{2,1,0:T(2,128)(2,1)}), bf16[32,2,16384]{2,1,0:T(2,128)(2,1)}, u32[]{:S(2)}, u32[]{:S(2)}) async-start(bf16[32,2,16384]{2,1,0:T(2,128)(2,1)} %reshape.121), calls=%async_computation.1 | async-start | bytes 4194304 | tf_op jit(solution)/shard_map/all_to_all | solution.py:65
  98.0 61.5 %all-to-all-start = ((bf16[16,512,128]{2,1,0:T(8,128)(2,1)}), bf16[16,512,128]{2,1,0:T(8,128)(2,1)}, u32[]{:S(2)}, u32[]{:S(2)}) async-start(bf16[16,512,128]{2,1,0:T(8,128)(2,1)} %bitcast.92), calls=%async_computation | async-start | bytes 4194304 | tf_op jit(solution)/shard_map/all_to_all | solution.py:20
  105.2 4.5 %copy-start.4 = (bf16[512,128]{1,0:T(8,128)(2,1)S(1)}, bf16[512,128]{1,0:T(8,128)(2,1)}, u32[]{:S(2)}) copy-start(bf16[512,128]{1,0:T(8,128)(2,1)} %param.11) | copy-start | bytes 393220
  105.2 74.1 %all-gather.2.cloned.1.call-start = ((), (), s32[]{:S(2)}) async-start(), calls=%async_computation.6 | async-start | bytes 2228224 | tf_op jit(solution)/shard_map/all_gather | solution.py:10
  121.1 4.9 %copy-start.3 = (bf16[512,512]{1,0:T(8,128)(2,1)S(1)}, bf16[512,512]{1,0:T(8,128)(2,1)}, u32[]{:S(2)}) copy-start(bf16[512,512]{1,0:T(8,128)(2,1)} %param.7) | copy-start | bytes 1572868
  125.7 0.9 copy-start.5
  161.8 54.6 %all-to-all-start.3 = ((bf16[16,512,128]{1,2,0:T(8,128)(2,1)}), bf16[16,512,128]{1,2,0:T(8,128)(2,1)}, u32[]{:S(2)}, u32[]{:S(2)}) async-start(bf16[16,512,128]{1,2,0:T(8,128)(2,1)} %stack.2), calls=%async_computation.3 | async-start | bytes 4194304 | tf_op jit(solution)/shard_map/all_to_all | solution.py:93
  216.4 22.1 %all-to-all-start.5 = ((bf16[32,2,4096]{2,1,0:T(2,128)(2,1)}), bf16[32,2,4096]{2,1,0:T(2,128)(2,1)}, u32[]{:S(2)}, u32[]{:S(2)}) async-start(bf16[32,2,4096]{2,1,0:T(2,128)(2,1)} %reshape.125), calls=%async_computation.5 | async-start | bytes 1048576 | tf_op jit(solution)/shard_map/all_to_all | solution.py:124
  238.5 55.9 %all-to-all-start.4 = ((bf16[32,2,16384]{2,1,0:T(2,128)(2,1)}), bf16[32,2,16384]{2,1,0:T(2,128)(2,1)}, u32[]{:S(2)}, u32[]{:S(2)}) async-start(bf16[32,2,16384]{2,1,0:T(2,128)(2,1)} %reshape.123), calls=%async_computation.4 | async-start | bytes 4194304 | tf_op jit(solution)/shard_map/all_to_all | solution.py:123
Sparse Core Ops, SparseCore 0:
  127.5 51.7 all-gather.1
